TPU v7x, 128 devices: a whole 4x4x4 slice. The times are simulated.
128 devices in a mesh: fsdp: 16 (over y, z), tp: 8 (over x, core).
Axes of the slice: x: 4, y: 4, z: 4, core: 2. Of those that a mesh axis runs over, the one named last changes fastest.
Arguments:
- tokens: bfloat16 [4096, 4096], P('fsdp', 'tp'), may hold values from -6 to 6
- gate_tiles: bfloat16 [288, 1024, 128], P('fsdp', 'tp'), may hold values from -0.125 to 0.125
- up_tiles: bfloat16 [288, 1024, 128], P('fsdp', 'tp'), may hold values from -0.125 to 0.125
- gate_slots: int32 [288, 8], P(None, 'tp'), may hold values from -1 to 27, as said below
- up_slots: int32 [288, 8], P(None, 'tp'), may hold values from -1 to 27, as said below
- cotangent: bfloat16 [4096, 14336], P('fsdp', 'tp'), may hold values from -6 to 6
Outputs:
- hidden: bfloat16 [4096, 14336], P('fsdp', 'tp')
- input_grad: bfloat16 [4096, 4096], P('fsdp', 'tp')
- gate_tile_grad: bfloat16 [288, 1024, 128], P('fsdp', 'tp')
- up_tile_grad: bfloat16 [288, 1024, 128], P('fsdp', 'tp')
Inputs may be any that keep to these rules, and one draw needn't show every extreme that they name: `gate_slots`: for each owner (rows f * 18 to (f + 1) * 18 - 1, column t) the non-negative entries are distinct positions of that owner, stand before its -1 entries, and number 10 to 18; in every draw some owner fills all 18 slots. `up_slots`: as for gate_slots, drawn independently.
All inputs are finite; a program needn't handle non-finite values.
Results may differ from a plain program's by a relative error of at most 0.02.
Values may be sent and summed in bfloat16 or wider, within the bound.
No kernel may reach another device: no remote copies, remote signals or barrier semaphores. Data moves between devices by JAX's collectives and lax.ppermute only.
A program may use at most 192 MiB of HBM per device.

v0:
```python
import jax
import jax.numpy as jnp
from jax import lax
from jax.sharding import PartitionSpec as P


def per_device(tokens, gate_tiles, up_tiles, gate_slots, up_slots, cotangent):
    n_fsdp = lax.axis_size("fsdp")
    n_tp = lax.axis_size("tp")
    tile_size = gate_tiles.shape[-1]
    capacity = gate_tiles.shape[0]
    tok_rows = tokens.shape[0]
    gathered = lax.all_gather(tokens, "tp", axis=1, tiled=True)
    model_width = gathered.shape[1]
    ff_local = cotangent.shape[1]
    row_tiles = model_width // (tile_size * n_fsdp)
    col_tiles = ff_local // tile_size
    owner_tiles = row_tiles * col_tiles
    positions = jnp.arange(owner_tiles, dtype=jnp.int32)
    gate_table = gate_slots.reshape(n_fsdp, capacity)
    up_table = up_slots.reshape(n_fsdp, capacity)

    def selector(table, kind):
        picks = (table[:, :, None] == positions).astype(kind)
        return picks.reshape(table.shape[0], table.shape[1], row_tiles, col_tiles)

    gate_select = selector(gate_table, jnp.bfloat16)
    up_select = selector(up_table, jnp.bfloat16)
    gate_all, up_all = (
        lax.all_gather(gate_tiles, "fsdp", axis=0, tiled=True),
        lax.all_gather(up_tiles, "fsdp", axis=0, tiled=True),
    )

    def unpack(blocks, select):
        dense_tiles = jnp.einsum(
            "fcrj,fcab->frjab",
            select,
            blocks.reshape(n_fsdp, capacity, tile_size, tile_size),
            preferred_element_type=jnp.float32,
        )
        return dense_tiles.astype(jnp.bfloat16)

    w_gate = unpack(gate_all, gate_select)
    w_up = unpack(up_all, up_select)
    token_view = gathered.reshape(tok_rows, n_fsdp, row_tiles, tile_size)
    gate = jnp.einsum(
        "tfra,frjab->tjb", token_view, w_gate, preferred_element_type=jnp.float32
    ).reshape(tok_rows, ff_local)
    up = jnp.einsum(
        "tfra,frjab->tjb", token_view, w_up, preferred_element_type=jnp.float32
    ).reshape(tok_rows, ff_local)
    sigmoid_gate = jax.nn.sigmoid(gate)
    activated = gate * sigmoid_gate
    hidden = (activated * up).astype(jnp.bfloat16)
    upstream = cotangent.astype(jnp.float32)
    gate_grad = (upstream * up * sigmoid_gate * (1.0 + gate * (1.0 - sigmoid_gate))).astype(
        jnp.bfloat16
    )
    up_grad = (upstream * activated).astype(jnp.bfloat16)
    gate_view = gate_grad.reshape(tok_rows, col_tiles, tile_size)
    up_view = up_grad.reshape(tok_rows, col_tiles, tile_size)
    total = jnp.einsum(
        "frjab,tjb->frat", w_gate, gate_view, preferred_element_type=jnp.float32
    ) + jnp.einsum("frjab,tjb->frat", w_up, up_view, preferred_element_type=jnp.float32)
    input_part = lax.psum_scatter(
        total.reshape(model_width // n_tp * lax.axis_size("tp"), tok_rows).astype(jnp.bfloat16),
        "tp",
        scatter_dimension=0,
        tiled=True,
    ).astype(jnp.float32)
    input_grad = input_part.T.astype(jnp.bfloat16)
    gate_dense = jnp.einsum(
        "tfra,tjb->frajb", token_view, gate_view, preferred_element_type=jnp.float32
    ).astype(jnp.bfloat16)
    up_dense = jnp.einsum(
        "tfra,tjb->frajb", token_view, up_view, preferred_element_type=jnp.float32
    ).astype(jnp.bfloat16)
    gate_packed = jnp.einsum(
        "fcrj,frajb->fcab", gate_select, gate_dense, preferred_element_type=jnp.float32
    )
    up_packed = jnp.einsum(
        "fcrj,frajb->fcab", up_select, up_dense, preferred_element_type=jnp.float32
    )
    gate_packed = gate_packed.reshape(capacity * lax.axis_size("fsdp"), tile_size, tile_size)
    up_packed = up_packed.reshape(capacity * lax.axis_size("fsdp"), tile_size, tile_size)
    summed = lax.psum_scatter(
        jnp.concatenate([gate_packed, up_packed], axis=2).astype(jnp.bfloat16),
        "fsdp",
        scatter_dimension=0,
        tiled=True,
    ).astype(jnp.float32)
    gate_tile_grad = summed[:, :, :tile_size].astype(jnp.bfloat16)
    up_tile_grad = summed[:, :, tile_size:].astype(jnp.bfloat16)
    return (hidden, input_grad, gate_tile_grad, up_tile_grad)


def solution(mesh):
    placed = (
        P("fsdp", "tp"),
        P("fsdp", "tp", None),
        P("fsdp", "tp", None),
        P(None, "tp"),
        P(None, "tp"),
        P("fsdp", "tp"),
    )
    return jax.shard_map(
        per_device,
        mesh=mesh,
        in_specs=placed,
        out_specs=(P("fsdp", "tp"), P("fsdp", "tp"), P("fsdp", "tp", None), P("fsdp", "tp", None)),
        check_vma=False,
    )
```

profile of v0, /device:TPU:0, one launch (start us, length us, event | category | flops | bytes accessed | tf_op | source)
XLA Modules:
  0.0 513.8 jit_solution(2433849524178457601)
XLA Ops:
  12.1 2.2 copy.67
  14.3 74.0 %all-gather.4.cloned.1.call-done = bf16[288,128,128]{2,1,0:T(8,128)(2,1)} async-done(((bf16[18,128,128]{2,1,0:T(8,128)(2,1)}), bf16[288,128,128]{2,1,0:T(8,128)(2,1)}) %all-gather.4.cloned.1.call-update) | async-done | bytes 9437200 | tf_op jit(solution)/shard_map/all_gather | solution.py:30
  88.4 16.0 %fusion.2 = bf16[16,2,14,128,128]{4,2,3,1,0:T(8,128)(2,1)} fusion(bf16[16,18,128,128,1]{3,2,1,0,4:T(8,128)(2,1)} %bitcast.119, s32[2,14]{1,0:T(2,128)S(1)} %multiply_add_fusion, s32[16,18]{1,0:T(8,128)S(1)} %eq.42), kind=kOutput, calls=%fused_computation.9 | convolution fusion | flops 264249216 | bytes 24118512 | tf_op jit(solution)/shard_map/fcrj,fcab->frjab/dot_general | solution.py:35
  104.4 11.0 %all-gather.6.cloned.1.call-done = bf16[256,4096]{0,1:T(8,128)(2,1)} async-done(((bf16[256,512]{0,1:T(8,128)(2,1)}), bf16[256,4096]{0,1:T(8,128)(2,1)}) %all-gather.6.cloned.1.call-update) | async-done | bytes 2097168 | tf_op jit(solution)/shard_map/all_gather | solution.py:13
  115.4 14.4 %fusion.6 = f32[14,128,256,1,1]{2,1,0,4,3:T(8,128)} fusion(bf16[256,16,2,128,1]{0,3,4,2,1:T(8,128)(2,1)} %bitcast.121, bf16[16,2,14,128,128]{4,2,3,1,0:T(8,128)(2,1)} %fusion.2), kind=kOutput, calls=%fused_computation.14 | convolution fusion | flops 3758096384 | bytes 18612224 | tf_op jit(solution)/shard_map/tfra,frjab->tjb/dot_general | solution.py:46
  129.8 63.8 %all-gather.8.cloned.1.call-done = bf16[288,128,128]{2,1,0:T(8,128)(2,1)} async-done(((bf16[18,128,128]{2,1,0:T(8,128)(2,1)}), bf16[288,128,128]{2,1,0:T(8,128)(2,1)}) %all-gather.8.cloned.1.call-update) | async-done | bytes 9437200 | tf_op jit(solution)/shard_map/all_gather | solution.py:31
  193.6 15.7 %fusion = bf16[16,2,14,128,128]{4,2,3,1,0:T(8,128)(2,1)} fusion(bf16[16,18,128,128,1]{3,2,1,0,4:T(8,128)(2,1)} %bitcast.120, s32[16,18]{1,0:T(8,128)S(1)} %eq.49, s32[2,14]{1,0:T(2,128)S(1)} %multiply_add_fusion), kind=kOutput, calls=%fused_computation.7 | convolution fusion | flops 264249216 | bytes 24118512 | tf_op jit(solution)/shard_map/fcrj,fcab->frjab/dot_general | solution.py:35
  209.4 13.6 %fusion.8 = f32[14,128,256,1,1]{2,1,0,4,3:T(8,128)S(1)} fusion(bf16[256,16,2,128,1]{0,3,4,2,1:T(8,128)(2,1)S(1)} %bitcast.122, bf16[16,2,14,128,128]{4,2,3,1,0:T(8,128)(2,1)} %fusion), kind=kOutput, calls=%fused_computation.16 | convolution fusion | flops 3758096384 | bytes 18612224 | tf_op jit(solution)/shard_map/tfra,frjab->tjb/dot_general | solution.py:49
  223.0 2.4 fusion.11
  225.3 7.2 %convert_bitcast_fusion = bf16[16,2,128,14,128]{2,4,1,0,3:T(8,128)(2,1)} fusion(bf16[256,14,128,1,1]{0,2,4,3,1:T(8,128)(2,1)S(1)} %bitcast.125, bf16[256,16,2,128,1]{0,3,2,1,4:T(8,128)(2,1)S(1)} %bitcast.123), kind=kOutput, calls=%fused_computation.5 | convolution fusion | flops 3765436416 | bytes 17694720 | tf_op jit(solution)/shard_map/tfra,tjb->frajb/dot_general | solution.py:75
  232.5 24.7 %copy.75 = bf16[16,2,128,14,128]{4,3,1,2,0:T(8,128)(2,1)} copy(bf16[16,2,128,14,128]{2,4,1,0,3:T(8,128)(2,1)} %convert_bitcast_fusion) | data formatting | bytes 29360128 | tf_op jit(solution)/shard_map/convert_element_type | solution.py:77
  257.2 10.2 %bitcast_convert_fusion = bf16[16,18,128,128]{3,1,2,0:T(8,128)(2,1)} fusion(bf16[16,2,128,14,128]{4,3,1,2,0:T(8,128)(2,1)} %copy.75, s32[16,18]{1,0:T(8,128)S(1)} %eq.49, s32[2,14]{1,0:T(2,128)S(1)} %multiply_add_fusion), kind=kOutput, calls=%fused_computation.2 | convolution fusion | flops 268967808 | bytes 24118512 | tf_op jit(solution)/shard_map/fcrj,frajb->fcab/dot_general | solution.py:81
  267.5 11.0 %copy.76 = bf16[16,18,128,128]{3,2,1,0:T(8,128)(2,1)} copy(bf16[16,18,128,128]{3,1,2,0:T(8,128)(2,1)} %bitcast_convert_fusion) | data formatting | bytes 18874368 | tf_op jit(solution)/shard_map/convert.4
  278.4 8.6 %convert_bitcast_fusion.1 = bf16[16,2,128,14,128]{2,4,1,0,3:T(8,128)(2,1)} fusion(bf16[256,14,128,1,1]{0,2,4,3,1:T(8,128)(2,1)} %bitcast.127, bf16[256,16,2,128,1]{0,3,2,1,4:T(8,128)(2,1)S(1)} %bitcast.124), kind=kOutput, calls=%fused_computation.6 | convolution fusion | flops 3765436416 | bytes 17694720 | tf_op jit(solution)/shard_map/tfra,tjb->frajb/dot_general | solution.py:72
  287.1 24.7 %copy.72 = bf16[16,2,128,14,128]{4,3,1,2,0:T(8,128)(2,1)} copy(bf16[16,2,128,14,128]{2,4,1,0,3:T(8,128)(2,1)} %convert_bitcast_fusion.1) | data formatting | bytes 29360128 | tf_op jit(solution)/shard_map/convert_element_type | solution.py:74
  311.8 10.4 %bitcast_convert_fusion.1 = bf16[16,18,128,128]{3,1,2,0:T(8,128)(2,1)} fusion(bf16[16,2,128,14,128]{4,3,1,2,0:T(8,128)(2,1)} %copy.72, s32[2,14]{1,0:T(2,128)S(1)} %multiply_add_fusion, s32[16,18]{1,0:T(8,128)S(1)} %eq.42), kind=kOutput, calls=%fused_computation.3 | convolution fusion | flops 268967808 | bytes 24118512 | tf_op jit(solution)/shard_map/fcrj,frajb->fcab/dot_general | solution.py:78
  322.2 11.0 %copy.73 = bf16[16,18,128,128]{3,2,1,0:T(8,128)(2,1)} copy(bf16[16,18,128,128]{3,1,2,0:T(8,128)(2,1)} %bitcast_convert_fusion.1) | data formatting | bytes 18874368 | tf_op jit(solution)/shard_map/convert.5
  333.2 16.8 %pad_maximum_fusion = bf16[288,128,256]{2,1,0:T(8,128)(2,1)} fusion(bf16[288,128,128]{2,1,0:T(8,128)(2,1)} %bitcast.117, bf16[288,128,128]{2,1,0:T(8,128)(2,1)} %bitcast.118), kind=kLoop, calls=%fused_computation.4 | loop fusion | flops 37748736 | bytes 37748736 | tf_op jit(solution)/shard_map/concatenate | solution.py:87
  351.2 9.3 %fusion.5 = f32[16,2,128,256,1]{3,2,4,1,0:T(8,128)S(1)} fusion(bf16[256,14,128,1,1]{0,2,1,4,3:T(8,128)(2,1)S(1)} %bitcast.128, bf16[16,2,14,128,128]{4,2,3,1,0:T(8,128)(2,1)} %fusion.2), kind=kOutput, calls=%fused_computation.13 | convolution fusion | flops 3758096384 | bytes 19791872 | tf_op jit(solution)/shard_map/frjab,tjb->frat/dot_general | solution.py:62
  360.5 10.7 %fusion.4 = bf16[16,2,128,256]{3,2,1,0:T(8,128)(2,1)} fusion(f32[16,2,128,256,1]{3,2,4,1,0:T(8,128)S(1)} %fusion.5, bf16[256,14,128,1,1]{0,2,1,4,3:T(8,128)(2,1)S(1)} %bitcast.126, bf16[16,2,14,128,128]{4,2,3,1,0:T(8,128)(2,1)} %fusion), kind=kOutput, calls=%fused_computation.12 | convolution fusion | flops 3760193536 | bytes 21889024 | tf_op jit(solution)/shard_map/frjab,tjb->frat/dot_general | solution.py:64
  371.2 4.1 copy.70
  376.7 94.2 %reduce-scatter.5.cloned.1.call-done = bf16[18,128,256]{2,1,0:T(8,128)(2,1)} async-done(((bf16[288,128,256]{2,1,0:T(8,128)(2,1)}), bf16[18,128,256]{2,1,0:T(8,128)(2,1)}) %reduce-scatter.5.cloned.1.call-update) | async-done | bytes 1179664 | tf_op jit(solution)/shard_map/reduce_scatter | solution.py:86
  470.9 2.4 fusion.26
  473.3 33.8 %reduce-scatter.3.cloned.1.call-done = bf16[512,256]{0,1:T(8,128)(2,1)} async-done(((bf16[4096,256]{0,1:T(8,128)(2,1)}), bf16[512,256]{0,1:T(8,128)(2,1)}) %reduce-scatter.3.cloned.1.call-update) | async-done | bytes 262160 | tf_op jit(solution)/shard_map/reduce_scatter | solution.py:65
  (27 shorter events, 7.5 us)
Async XLA Ops:
  7.2 81.2 %all-gather.4.cloned.1.call-start = ((), (), s32[]{:S(2)}) async-start(), calls=%async_computation.2 | async-start | bytes 10027008 | tf_op jit(solution)/shard_map/all_gather | solution.py:30
  7.9 107.5 %all-gather.6.cloned.1.call-start = ((), (), s32[]{:S(2)}) async-start(), calls=%async_computation.3 | async-start | bytes 2359296 | tf_op jit(solution)/shard_map/all_gather | solution.py:13
  9.8 183.9 %all-gather.8.cloned.1.call-start = ((), (), s32[]{:S(2)}) async-start(), calls=%async_computation.4 | async-start | bytes 10027008 | tf_op jit(solution)/shard_map/all_gather | solution.py:31
  10.5 460.4 %reduce-scatter.5.cloned.1.call-start = ((), (), s32[]{:S(2)}) async-start(), calls=%async_computation.6 | async-start | bytes 20054016 | tf_op jit(solution)/shard_map/reduce_scatter | solution.py:86
  193.6 15.7 %copy-start = (bf16[256,4096]{0,1:T(8,128)(2,1)S(1)}, bf16[256,4096]{0,1:T(8,128)(2,1)}, u32[]{:S(2)}) copy-start(bf16[256,4096]{0,1:T(8,128)(2,1)} %all-gather.6.cloned.1.call-done) | copy-start | bytes 6291460
  209.4 13.6 %copy-start.3 = (bf16[256,1792]{0,1:T(8,128)(2,1)S(1)}, bf16[256,1792]{0,1:T(8,128)(2,1)}, u32[]{:S(2)}) copy-start(bf16[256,1792]{0,1:T(8,128)(2,1)} %copy.67) | copy-start | bytes 2752516
  209.4 13.6 %copy-start.4 = (f32[14,128,256,1,1]{2,1,0,4,3:T(8,128)S(1)}, f32[14,128,256,1,1]{2,1,0,4,3:T(8,128)}, u32[]{:S(2)}) copy-start(f32[14,128,256,1,1]{2,1,0,4,3:T(8,128)} %fusion.6) | copy-start | bytes 5505028
  350.0 1.2 copy-start.1
  350.0 157.1 %reduce-scatter.3.cloned.1.call-start = ((), (), s32[]{:S(2)}) async-start(), calls=%async_computation.5 | async-start | bytes 2359296 | tf_op jit(solution)/shard_map/reduce_scatter | solution.py:65
  360.5 14.9 %copy-start.2 = (bf16[256,1792]{0,1:T(8,128)(2,1)S(1)}, bf16[256,1792]{0,1:T(8,128)(2,1)}, u32[]{:S(2)}) copy-start(bf16[256,1792]{0,1:T(8,128)(2,1)} %get-tuple-element.17) | copy-start | bytes 2752516
Sparse Core Ops, SparseCore 0:
  10.2 78.1 all-gather.3
  90.7 24.6 all-gather.5
  117.6 75.9 all-gather.7
  350.1 120.7 reduce-scatter.4
  473.8 33.2 reduce-scatter.2
where the time goes:
time: 520 us; the launch traced here: 514 us
  waiting for transfers between devices  278 us (53%)
  matrix products  116 us (22%)
  local copies, waits for them, and re-layouts  84.6 us (16%)
  other arithmetic  20.6 us (4%)
  between operations  14.1 us (3%)
    reduce_scatter x1, waiting for transfers between devices, per_device(): lax.psum_scatter(jnp.concatenate([gate_packed, up_packed], axis=2).astype...  94.2 us
    all_gather x1, waiting for transfers between devices, per_device(): lax.all_gather(gate_tiles, 'fsdp', axis=0, tiled=True)  74 us
    all_gather x1, waiting for transfers between devices, per_device(): lax.all_gather(up_tiles, 'fsdp', axis=0, tiled=True)  63.8 us
    reduce_scatter x1, waiting for transfers between devices, per_device(): lax.psum_scatter(total.reshape(model_width // n_tp * lax.axis_size('tp'),...  33.8 us
    dot_general x2, matrix products, unpack(): jnp.einsum('fcrj,fcab->frjab', select, blocks.reshape(n_fsdp, capacity, t...  31.8 us
    convert_element_type x1, local copies, waits for them, and re-layouts, per_device(): up_dense = jnp.einsum('tfra,tjb->frajb', token_view, up_view, preferred_e...  24.7 us
    convert_element_type x1, local copies, waits for them, and re-layouts, per_device(): gate_dense = jnp.einsum('tfra,tjb->frajb', token_view, gate_view, preferr...  24.7 us
    another operation x2, local copies, waits for them, and re-layouts  21.9 us
  transfers between devices with their start and end apart: 5, of which 5 were waited for; matrix products, arithmetic and copies ran while one was open for 12% of the time, Pallas kernels for 0%

commit v1 on v0

--- a/solution.py
+++ b/solution.py
@@ -10,7 +10,12 @@
     tile_size = gate_tiles.shape[-1]
     capacity = gate_tiles.shape[0]
     tok_rows = tokens.shape[0]
-    gathered = lax.all_gather(tokens, "tp", axis=1, tiled=True)
+    ring = [tokens]
+    for hop in range(7):
+        ring.append(lax.ppermute(ring[-1], "tp", [(dev, (dev + 1) % 8) for dev in range(8)]))
+    gathered = jnp.roll(
+        jnp.concatenate(ring[::-1], axis=1), (lax.axis_index("tp") + 1) * ring[0].shape[1], axis=1
+    )
     model_width = gathered.shape[1]
     ff_local = cotangent.shape[1]
     row_tiles = model_width // (tile_size * n_fsdp)

time: 520 us -> 498 us (0.958)
  waiting for transfers between devices: 278 us -> 247 us
  matrix products: 116 us -> 129 us
    ppermute x0 -> x7, waiting for transfers between devices: none -> 47.4 us  [per_device(): lax.ppermute(ring[-1], 'tp', [(dev, (dev + 1) % 8) for dev in range(8)])]
    dot_general x0 -> x2, local copies, waits for them, and re-layouts: none -> 47.4 us  [the longest x1 24.4 us: per_device(): jnp.einsum('tfra,frjab->tjb', token_view, w_gate, preferred_element_type=...]
    convert_element_type x2, local copies, waits for them, and re-layouts: 49.4 us -> 2.75 us  [the longest x1 1.45 us: per_device(): (upstream * up * sigmoid_gate * (1.0 + gate * (1.0 - sigmoid_gate))).asty...]
    all_gather x1, waiting for transfers between devices: 74 us -> 28.9 us  [per_device(): lax.all_gather(gate_tiles, 'fsdp', axis=0, tiled=True)]
    all_gather x1, waiting for transfers between devices: 63.8 us -> 37.5 us  [per_device(): lax.all_gather(up_tiles, 'fsdp', axis=0, tiled=True)]
    all_gather x1 -> x0, waiting for transfers between devices: 11 us -> none  [per_device(): gathered = lax.all_gather(tokens, 'tp', axis=1, tiled=True)]
    dot_general x1, matrix products: 10.2 us -> 18.2 us  [per_device(): jnp.einsum('fcrj,frajb->fcab', up_select, up_dense, preferred_element_typ...]
    dot_general x1, matrix products: 10.4 us -> 18.2 us  [per_device(): jnp.einsum('fcrj,frajb->fcab', gate_select, gate_dense, preferred_element...]
  transfers between devices with their start and end apart: 5 -> 11, of which waited for: 5 -> 11; matrix products, arithmetic and copies ran while one was open for 12% -> 14% of each run, Pallas kernels for 0% -> 0%
where the time goes in v1:
time: 498 us; the launch traced here: 488 us
  waiting for transfers between devices  247 us (50%)
  matrix products  129 us (26%)
  local copies, waits for them, and re-layouts  80.2 us (16%)
  other arithmetic  18.2 us (4%)
  between operations  14.2 us (3%)
    reduce_scatter x1, waiting for transfers between devices, per_device(): lax.psum_scatter(jnp.concatenate([gate_packed, up_packed], axis=2).astype...  97.7 us
    ppermute x7, waiting for transfers between devices, per_device(): lax.ppermute(ring[-1], 'tp', [(dev, (dev + 1) % 8) for dev in range(8)])  47.4 us
    all_gather x1, waiting for transfers between devices, per_device(): lax.all_gather(up_tiles, 'fsdp', axis=0, tiled=True)  37.5 us
    reduce_scatter x1, waiting for transfers between devices, per_device(): lax.psum_scatter(total.reshape(model_width // n_tp * lax.axis_size('tp'),...  33.7 us
    dot_general x2, matrix products, unpack(): jnp.einsum('fcrj,fcab->frjab', select, blocks.reshape(n_fsdp, capacity, t...  31.2 us
    all_gather x1, waiting for transfers between devices, per_device(): lax.all_gather(gate_tiles, 'fsdp', axis=0, tiled=True)  28.9 us
    dot_general x1, local copies, waits for them, and re-layouts, per_device(): jnp.einsum('tfra,frjab->tjb', token_view, w_gate, preferred_element_type=...  24.4 us
    dot_general x1, local copies, waits for them, and re-layouts, per_device(): jnp.einsum('tfra,frjab->tjb', token_view, w_up, preferred_element_type=jn...  23 us
  transfers between devices with their start and end apart: 11, of which 11 were waited for; matrix products, arithmetic and copies ran while one was open for 14% of the time, Pallas kernels for 0%

profile of v1, /device:TPU:0, one launch (start us, length us, event | category | flops | bytes accessed | tf_op | source)
XLA Modules:
  0.0 488.2 jit_solution(7904106828909276050)
XLA Ops:
  16.8 7.0 %collective-permute-done.1 = bf16[256,512]{0,1:T(8,128)(2,1)S(1)} collective-permute-done((bf16[256,512]{0,1:T(8,128)(2,1)S(1)}, bf16[256,512]{0,1:T(8,128)(2,1)S(1)}, u32[]{:S(2)}, u32[]{:S(2)}) %collective-permute-start.1) | collective-permute-done | bytes 262176 | tf_op jit(solution)/shard_map/ppermute | solution.py:15
  23.8 7.0 %collective-permute-done.2 = bf16[256,512]{0,1:T(8,128)(2,1)S(1)} collective-permute-done((bf16[256,512]{0,1:T(8,128)(2,1)S(1)}, bf16[256,512]{0,1:T(8,128)(2,1)S(1)}, u32[]{:S(2)}, u32[]{:S(2)}) %collective-permute-start.2) | collective-permute-done | bytes 262176 | tf_op jit(solution)/shard_map/ppermute | solution.py:15
  30.8 7.0 %collective-permute-done.3 = bf16[256,512]{0,1:T(8,128)(2,1)S(1)} collective-permute-done((bf16[256,512]{0,1:T(8,128)(2,1)S(1)}, bf16[256,512]{0,1:T(8,128)(2,1)S(1)}, u32[]{:S(2)}, u32[]{:S(2)}) %collective-permute-start.3) | collective-permute-done | bytes 262176 | tf_op jit(solution)/shard_map/ppermute | solution.py:15
  37.8 7.0 %collective-permute-done.4 = bf16[256,512]{0,1:T(8,128)(2,1)S(1)} collective-permute-done((bf16[256,512]{0,1:T(8,128)(2,1)S(1)}, bf16[256,512]{0,1:T(8,128)(2,1)S(1)}, u32[]{:S(2)}, u32[]{:S(2)}) %collective-permute-start.4) | collective-permute-done | bytes 262176 | tf_op jit(solution)/shard_map/ppermute | solution.py:15
  44.8 7.0 %collective-permute-done.5 = bf16[256,512]{0,1:T(8,128)(2,1)S(1)} collective-permute-done((bf16[256,512]{0,1:T(8,128)(2,1)S(1)}, bf16[256,512]{0,1:T(8,128)(2,1)S(1)}, u32[]{:S(2)}, u32[]{:S(2)}) %collective-permute-start.5) | collective-permute-done | bytes 262176 | tf_op jit(solution)/shard_map/ppermute | solution.py:15
  59.4 28.9 %all-gather.3.cloned.1.call-done = bf16[288,128,128]{2,1,0:T(8,128)(2,1)} async-done(((bf16[18,128,128]{2,1,0:T(8,128)(2,1)}), bf16[288,128,128]{2,1,0:T(8,128)(2,1)}) %all-gather.3.cloned.1.call-update) | async-done | bytes 9437200 | tf_op jit(solution)/shard_map/all_gather | solution.py:35
  88.4 15.6 %fusion.12 = bf16[16,2,14,128,128]{4,2,3,1,0:T(8,128)(2,1)} fusion(bf16[16,18,128,128,1]{3,2,1,0,4:T(8,128)(2,1)} %bitcast.83, s32[2,14]{1,0:T(2,128)S(1)} %multiply_add_fusion, s32[16,18]{1,0:T(8,128)S(1)} %eq.45), kind=kOutput, calls=%fused_computation.15 | convolution fusion | flops 271589248 | bytes 24118512 | tf_op jit(solution)/shard_map/fcrj,fcab->frjab/dot_general | solution.py:40
  104.0 24.4 %copy.82 = bf16[14,128,128,16,2]{2,1,0,4,3:T(8,128)(2,1)} copy(bf16[14,128,128,16,2]{1,0,2,4,3:T(8,128)(2,1)} %bitcast.79) | data formatting | bytes 29360128 | tf_op jit(solution)/shard_map/tfra,frjab->tjb/dot_general | solution.py:51
  128.3 37.5 %all-gather.5.cloned.1.call-done = bf16[288,128,128]{2,1,0:T(8,128)(2,1)} async-done(((bf16[18,128,128]{2,1,0:T(8,128)(2,1)}), bf16[288,128,128]{2,1,0:T(8,128)(2,1)}) %all-gather.5.cloned.1.call-update) | async-done | bytes 9437200 | tf_op jit(solution)/shard_map/all_gather | solution.py:36
  165.9 15.6 %fusion.15 = bf16[16,2,14,128,128]{4,2,3,1,0:T(8,128)(2,1)} fusion(bf16[16,18,128,128,1]{3,2,1,0,4:T(8,128)(2,1)} %bitcast.84, s32[16,18]{1,0:T(8,128)S(1)} %eq.52, s32[2,14]{1,0:T(2,128)S(1)} %multiply_add_fusion), kind=kOutput, calls=%fused_computation.16 | convolution fusion | flops 271589248 | bytes 24118512 | tf_op jit(solution)/shard_map/fcrj,fcab->frjab/dot_general | solution.py:40
  181.4 23.0 %copy.85 = bf16[14,128,128,16,2]{2,1,0,4,3:T(8,128)(2,1)} copy(bf16[14,128,128,16,2]{1,0,2,4,3:T(8,128)(2,1)} %bitcast.80) | data formatting | bytes 29360128 | tf_op jit(solution)/shard_map/tfra,frjab->tjb/dot_general | solution.py:54
  204.5 9.1 %convolution_bitcast_fusion.1 = f32[256,1792]{1,0:T(8,128)} fusion(bf16[256,16,2,128]{0,3,2,1:T(8,128)(2,1)S(1)} %bitcast.85, bf16[1792,128,16,2]{1,0,3,2:T(8,128)(2,1)} %bitcast.89), kind=kOutput, calls=%fused_computation.22 | convolution fusion | flops 3758096384 | bytes 18612224 | tf_op jit(solution)/shard_map/tfra,frjab->tjb/dot_general | solution.py:51
  213.6 16.7 %fusion.27 = (bf16[256,1792]{1,0:T(8,128)(2,1)}, bf16[256,1792]{1,0:T(8,128)(2,1)}, bf16[256,1792]{1,0:T(8,128)(2,1)S(1)}) fusion(bf16[256,1792]{1,0:T(8,128)(2,1)} %param.11, f32[256,1792]{1,0:T(8,128)} %convolution_bitcast_fusion.1, bf16[256,16,2,128]{0,3,2,1:T(8,128)(2,1)S(1)} %bitcast.86, bf16[1792,128,16,2]{1,0,3,2:T(8,128)(2,1)} %bitcast.90), kind=kOutput, calls=%fused_computation.27 | convolution fusion | flops 3765436416 | bytes 22282240 | tf_op jit(solution)/shard_map/tfra,frjab->tjb/dot_general | solution.py:54
  233.0 8.4 %convolution_convert_fusion = bf16[16,2,128,14,128]{4,2,3,1,0:T(8,128)(2,1)} fusion(bf16[256,16,2,128,1]{0,3,4,2,1:T(8,128)(2,1)S(1)} %bitcast.87, bf16[256,14,128,1,1]{0,2,1,4,3:T(8,128)(2,1)} %bitcast.93), kind=kOutput, calls=%fused_computation.17 | convolution fusion | flops 3765436416 | bytes 17694720 | tf_op jit(solution)/shard_map/tfra,tjb->frajb/dot_general | solution.py:80
  241.4 18.2 %bitcast_convert_fusion = bf16[16,18,128,128]{3,1,2,0:T(8,128)(2,1)} fusion(bf16[16,2,128,14,128]{4,2,3,1,0:T(8,128)(2,1)} %convolution_convert_fusion, s32[16,18]{1,0:T(8,128)S(1)} %eq.52, s32[2,14]{1,0:T(2,128)S(1)} %multiply_add_fusion), kind=kOutput, calls=%fused_computation | convolution fusion | flops 268967808 | bytes 24118512 | tf_op jit(solution)/shard_map/fcrj,frajb->fcab/dot_general | solution.py:86
  259.6 11.0 %copy.60 = bf16[16,18,128,128]{3,2,1,0:T(8,128)(2,1)} copy(bf16[16,18,128,128]{3,1,2,0:T(8,128)(2,1)} %bitcast_convert_fusion) | data formatting | bytes 18874368 | tf_op jit(solution)/shard_map/convert.4
  270.6 7.7 %convolution_convert_fusion.1 = bf16[16,2,128,14,128]{4,2,3,1,0:T(8,128)(2,1)} fusion(bf16[256,16,2,128,1]{0,3,4,2,1:T(8,128)(2,1)S(1)} %bitcast.88, bf16[256,14,128,1,1]{0,2,1,4,3:T(8,128)(2,1)S(1)} %bitcast.91), kind=kOutput, calls=%fused_computation.18 | convolution fusion | flops 3765436416 | bytes 17694720 | tf_op jit(solution)/shard_map/tfra,tjb->frajb/dot_general | solution.py:77
  278.3 18.2 %bitcast_convert_fusion.1 = bf16[16,18,128,128]{3,1,2,0:T(8,128)(2,1)} fusion(bf16[16,2,128,14,128]{4,2,3,1,0:T(8,128)(2,1)} %convolution_convert_fusion.1, s32[2,14]{1,0:T(2,128)S(1)} %multiply_add_fusion, s32[16,18]{1,0:T(8,128)S(1)} %eq.45), kind=kOutput, calls=%fused_computation.1 | convolution fusion | flops 268967808 | bytes 24118512 | tf_op jit(solution)/shard_map/fcrj,frajb->fcab/dot_general | solution.py:83
  296.5 11.0 %copy.57 = bf16[16,18,128,128]{3,2,1,0:T(8,128)(2,1)} copy(bf16[16,18,128,128]{3,1,2,0:T(8,128)(2,1)} %bitcast_convert_fusion.1) | data formatting | bytes 18874368 | tf_op jit(solution)/shard_map/convert.5
  307.5 16.8 %pad_maximum_fusion = bf16[288,128,256]{2,1,0:T(8,128)(2,1)} fusion(bf16[288,128,128]{2,1,0:T(8,128)(2,1)} %bitcast.81, bf16[288,128,128]{2,1,0:T(8,128)(2,1)} %bitcast.82), kind=kLoop, calls=%fused_computation.2 | loop fusion | flops 37748736 | bytes 37748736 | tf_op jit(solution)/shard_map/concatenate | solution.py:92
  325.5 9.5 %fusion.4 = f32[16,2,128,256,1]{3,2,4,1,0:T(8,128)S(1)} fusion(bf16[256,14,128,1,1]{0,2,1,4,3:T(8,128)(2,1)S(1)} %bitcast.94, bf16[16,2,14,128,128]{4,2,3,1,0:T(8,128)(2,1)} %fusion.15), kind=kOutput, calls=%fused_computation.7 | convolution fusion | flops 3758096384 | bytes 19791872 | tf_op jit(solution)/shard_map/frjab,tjb->frat/dot_general | solution.py:69
  335.0 9.6 %fusion.22 = bf16[16,2,128,256]{3,2,1,0:T(8,128)(2,1)S(1)} fusion(f32[16,2,128,256,1]{3,2,4,1,0:T(8,128)S(1)} %fusion.4, bf16[256,14,128,1,1]{0,2,1,4,3:T(8,128)(2,1)S(1)} %bitcast.92, bf16[16,2,14,128,128]{4,2,3,1,0:T(8,128)(2,1)} %fusion.12), kind=kOutput, calls=%fused_computation.20 | convolution fusion | flops 3760193536 | bytes 21889024 | tf_op jit(solution)/shard_map/frjab,tjb->frat/dot_general | solution.py:67
  347.6 97.7 %reduce-scatter.5.cloned.1.call-done = bf16[18,128,256]{2,1,0:T(8,128)(2,1)} async-done(((bf16[288,128,256]{2,1,0:T(8,128)(2,1)}), bf16[18,128,256]{2,1,0:T(8,128)(2,1)}) %reduce-scatter.5.cloned.1.call-update) | async-done | bytes 1179664 | tf_op jit(solution)/shard_map/reduce_scatter | solution.py:91
  447.7 33.7 %reduce-scatter.3.cloned.1.call-done = bf16[512,256]{0,1:T(8,128)(2,1)} async-done(((bf16[4096,256]{0,1:T(8,128)(2,1)}), bf16[512,256]{0,1:T(8,128)(2,1)}) %reduce-scatter.3.cloned.1.call-update) | async-done | bytes 262160 | tf_op jit(solution)/shard_map/reduce_scatter | solution.py:70
  (46 shorter events, 26.3 us)
Async XLA Ops:
  7.2 81.2 %all-gather.3.cloned.1.call-start = ((), (), s32[]{:S(2)}) async-start(), calls=%async_computation.2 | async-start | bytes 10027008 | tf_op jit(solution)/shard_map/all_gather | solution.py:35
  7.9 158.0 %all-gather.5.cloned.1.call-start = ((), (), s32[]{:S(2)}) async-start(), calls=%async_computation.3 | async-start | bytes 10027008 | tf_op jit(solution)/shard_map/all_gather | solution.py:36
  8.6 436.6 %reduce-scatter.5.cloned.1.call-start = ((), (), s32[]{:S(2)}) async-start(), calls=%async_computation.5 | async-start | bytes 20054016 | tf_op jit(solution)/shard_map/reduce_scatter | solution.py:91
  9.8 7.0 %collective-permute-start = (bf16[256,512]{0,1:T(8,128)(2,1)S(1)}, bf16[256,512]{0,1:T(8,128)(2,1)S(1)}, u32[]{:S(2)}, u32[]{:S(2)}) collective-permute-start(bf16[256,512]{0,1:T(8,128)(2,1)S(1)} %copy.37), channel_id=1, source_target_pairs={{0,1},{1,2},{2,3},{3,4},{4,5},{5,6},{6,7},{7,0},{8,9},{9,10},{10,1... | collective-permute-start | bytes 786440 | tf_op jit(solution)/shard_map/ppermute | solution.py:15
  16.8 7.0 %collective-permute-start.1 = (bf16[256,512]{0,1:T(8,128)(2,1)S(1)}, bf16[256,512]{0,1:T(8,128)(2,1)S(1)}, u32[]{:S(2)}, u32[]{:S(2)}) collective-permute-start(bf16[256,512]{0,1:T(8,128)(2,1)S(1)} %collective-permute-done), channel_id=1, source_target_pairs={{0,1},{1,2},{2,3},{3,4},{4,5},{5,6},{6,7},{7,0},{8,9},{9,10},{10,1... | collective-permute-start | bytes 786440 | tf_op jit(solution)/shard_map/ppermute | solution.py:15
  23.8 7.0 %collective-permute-start.2 = (bf16[256,512]{0,1:T(8,128)(2,1)S(1)}, bf16[256,512]{0,1:T(8,128)(2,1)S(1)}, u32[]{:S(2)}, u32[]{:S(2)}) collective-permute-start(bf16[256,512]{0,1:T(8,128)(2,1)S(1)} %collective-permute-done.1), channel_id=1, source_target_pairs={{0,1},{1,2},{2,3},{3,4},{4,5},{5,6},{6,7},{7,0},{8,9},{9,10},{10,1... | collective-permute-start | bytes 786440 | tf_op jit(solution)/shard_map/ppermute | solution.py:15
  30.8 7.0 %collective-permute-start.3 = (bf16[256,512]{0,1:T(8,128)(2,1)S(1)}, bf16[256,512]{0,1:T(8,128)(2,1)S(1)}, u32[]{:S(2)}, u32[]{:S(2)}) collective-permute-start(bf16[256,512]{0,1:T(8,128)(2,1)S(1)} %collective-permute-done.2), channel_id=1, source_target_pairs={{0,1},{1,2},{2,3},{3,4},{4,5},{5,6},{6,7},{7,0},{8,9},{9,10},{10,1... | collective-permute-start | bytes 786440 | tf_op jit(solution)/shard_map/ppermute | solution.py:15
  37.8 7.0 %collective-permute-start.4 = (bf16[256,512]{0,1:T(8,128)(2,1)S(1)}, bf16[256,512]{0,1:T(8,128)(2,1)S(1)}, u32[]{:S(2)}, u32[]{:S(2)}) collective-permute-start(bf16[256,512]{0,1:T(8,128)(2,1)S(1)} %collective-permute-done.3), channel_id=1, source_target_pairs={{0,1},{1,2},{2,3},{3,4},{4,5},{5,6},{6,7},{7,0},{8,9},{9,10},{10,1... | collective-permute-start | bytes 786440 | tf_op jit(solution)/shard_map/ppermute | solution.py:15
  44.8 7.0 %collective-permute-start.5 = (bf16[256,512]{0,1:T(8,128)(2,1)S(1)}, bf16[256,512]{0,1:T(8,128)(2,1)S(1)}, u32[]{:S(2)}, u32[]{:S(2)}) collective-permute-start(bf16[256,512]{0,1:T(8,128)(2,1)S(1)} %collective-permute-done.4), channel_id=1, source_target_pairs={{0,1},{1,2},{2,3},{3,4},{4,5},{5,6},{6,7},{7,0},{8,9},{9,10},{10,1... | collective-permute-start | bytes 786440 | tf_op jit(solution)/shard_map/ppermute | solution.py:15
  51.8 7.0 %collective-permute-start.6 = (bf16[256,512]{0,1:T(8,128)(2,1)S(1)}, bf16[256,512]{0,1:T(8,128)(2,1)S(1)}, u32[]{:S(2)}, u32[]{:S(2)}) collective-permute-start(bf16[256,512]{0,1:T(8,128)(2,1)S(1)} %collective-permute-done.5), channel_id=1, source_target_pairs={{0,1},{1,2},{2,3},{3,4},{4,5},{5,6},{6,7},{7,0},{8,9},{9,10},{10,1... | collective-permute-start | bytes 786440 | tf_op jit(solution)/shard_map/ppermute | solution.py:15
  324.3 1.2 copy-start
  324.3 157.0 %reduce-scatter.3.cloned.1.call-start = ((), (), s32[]{:S(2)}) async-start(), calls=%async_computation.4 | async-start | bytes 2359296 | tf_op jit(solution)/shard_map/reduce_scatter | solution.py:70
Sparse Core Ops, SparseCore 0:
  10.2 78.1 all-gather.2
  90.6 75.2 all-gather.4
  324.5 120.7 reduce-scatter.4
  448.1 33.2 reduce-scatter.2
